TPU v7x, 32 devices: a whole 2x2x4 slice. The times are simulated.
32 devices in a mesh: dp: 16 (over z, y, core), tensor: 2 (over x).
Axes of the slice: x: 2, y: 2, z: 4, core: 2. Of those that a mesh axis runs over, the one named last changes fastest.
Arguments:
- block_in: bfloat16 [32768, 768], P('dp', 'tensor'), may hold values from -6 to 6
- cotangent: bfloat16 [32768, 768], P('dp', 'tensor'), may hold values from -6 to 6
- segments: int32 [32768], P('dp'), may hold values from 0 to 23, as said below
- w_qkv: bfloat16 [768, 3, 768], P('dp', None, 'tensor'), may hold values from -0.21875 to 0.21875
- w_attn_out: bfloat16 [768, 768], P('tensor', 'dp'), may hold values from -0.875 to 0.875
- w_mlp_in: bfloat16 [768, 2, 1152], P('dp', None, 'tensor'), may hold values from -0.21875 to 0.21875
- w_mlp_out: bfloat16 [1152, 768], P('tensor', 'dp'), may hold values from -0.25 to 0.25
- gain_attn: bfloat16 [768], P('dp'), may hold values from 0.099609375 to 1.8984375
- gain_mlp: bfloat16 [768], P('dp'), may hold values from 0.099609375 to 1.8984375
Outputs:
- block_out: bfloat16 [32768, 768], P('dp', 'tensor')
- grad_in: bfloat16 [32768, 768], P('dp', 'tensor')
- grad_qkv: float32 [768, 3, 768], P('dp', None, 'tensor')
- grad_attn_out: float32 [768, 768], P('tensor', 'dp')
- grad_mlp_in: float32 [768, 2, 1152], P('dp', None, 'tensor')
- grad_mlp_out: float32 [1152, 768], P('tensor', 'dp')
- grad_gain_attn: float32 [768], P(('dp', 'tensor'))
- grad_gain_mlp: float32 [768], P(('dp', 'tensor'))
Inputs may be any that keep to these rules, and one draw needn't show every extreme that they name: `segments`: document numbers never fall along the tokens; the tokens of sequence s (positions s * 4096 to s * 4096 + 4095) carry numbers 3 * s to 3 * s + 2 only, so no document crosses the end of a sequence.
All inputs are finite; a program needn't handle non-finite values.
Results may differ from a plain program's by a relative error of at most 0.023.
Values may be sent and summed in bfloat16 or wider, within the bound.
A program may use at most 384 MiB of HBM per device.

v0:
```python
import functools

import jax
import jax.numpy as jnp
from jax import lax
from jax.experimental import pallas as pl
from jax.experimental.pallas import tpu as pltpu
from jax.sharding import PartitionSpec as P

HEAD_DIM = 64

EPS = 1e-05
THETA = 160000.0
LOG2E = 1.4426950408889634
FACTOR = HEAD_DIM**-0.5 * LOG2E
MASKED = -1e30
VMEM_BYTES = 56 * 1024 * 1024


def swapped(block, axis, stride):
    count = lax.axis_size(axis)
    route = []
    for low in range(count):
        high = low | 1 << stride
        if high != low and high < count:
            route += [(low, high), (high, low)]
    return lax.ppermute(block, axis, route)


def exact_gelu(values):
    return jax.nn.gelu(values, approximate=False)


def statistics(values):
    centre = jnp.mean(values, axis=-1, keepdims=True)
    centred = values - centre
    inverse = lax.rsqrt(jnp.mean(centred * centred, axis=-1, keepdims=True) + EPS)
    return (centred * inverse, inverse)


def rotation(length, offset):
    half = HEAD_DIM // 2
    ladder = THETA ** (-(jnp.arange(half, dtype=jnp.float32) * 2.0 / HEAD_DIM))
    places = (offset + jnp.arange(length, dtype=jnp.int32)).astype(jnp.float32)
    angle = ladder[:, None] * places[None, :]
    return (jnp.cos(angle)[None], jnp.sin(angle)[None])


def turn(values, cosine, sine):
    half = values.shape[1] // 2
    former = values[:, :half]
    latter = values[:, half:]
    return jnp.concatenate(
        [former * cosine - latter * sine, latter * cosine + former * sine], axis=1
    )


def unturn(grads, cosine, sine):
    half = grads.shape[1] // 2
    former = grads[:, :half]
    latter = grads[:, half:]
    return jnp.concatenate(
        [former * cosine + latter * sine, latter * cosine - former * sine], axis=1
    )


def product(left, right, dims):
    return lax.dot_general(left, right, (dims, ((), ())), preferred_element_type=jnp.float32)


def attend_kernel(
    first_ref, last_ref, q_ref, k_ref, v_ref, qlab_ref, klab_ref, out_ref, lse_ref, keys, *, part
):
    block = pl.program_id(1)
    heads, dim, rows = q_ref.shape

    @pl.when(block == 0)
    def _():
        for h in range(heads):
            keys[h] = k_ref[h].T

    labels = qlab_ref[...]
    queries = [q_ref[h] for h in range(heads)]

    def step(j, carry):
        start = pl.multiple_of(j * part, part)
        same = klab_ref[pl.ds(start, part), :] == labels
        state = []
        for h in range(heads):
            highest, total, mixed = carry[h]
            raw = product(keys[h, pl.ds(start, part), :], queries[h], ((1,), (0,)))
            raw = jnp.where(same, raw, MASKED)
            peak = jnp.maximum(highest, jnp.max(raw, axis=0, keepdims=True))
            fade = jnp.exp2((highest - peak) * FACTOR)
            prob = jnp.exp2(raw * FACTOR - peak * FACTOR)
            total = total * fade + jnp.sum(prob, axis=0, keepdims=True)
            mixed = mixed * fade + product(
                v_ref[h, :, pl.ds(start, part)], prob.astype(jnp.bfloat16), ((1,), (0,))
            )
            state.append((peak, total, mixed))
        return tuple(state)

    empty = tuple(
        (
            jnp.full((1, rows), MASKED, jnp.float32),
            jnp.zeros((1, rows), jnp.float32),
            jnp.zeros((dim, rows), jnp.float32),
        )
        for _ in range(heads)
    )
    result = lax.fori_loop(first_ref[block], last_ref[block], step, empty)
    for h in range(heads):
        highest, total, mixed = result[h]
        out_ref[h] = (mixed / total).astype(out_ref.dtype)
        lse_ref[h] = highest * FACTOR + jnp.log2(total)


def attend_back_kernel(
    first_ref,
    last_ref,
    q_ref,
    k_ref,
    v_ref,
    out_ref,
    grad_ref,
    lse_ref,
    qlab_ref,
    klab_ref,
    dq_ref,
    dk_ref,
    dv_ref,
    keys,
    values,
    key_grad,
    value_grad,
    *,
    part,
):
    block = pl.program_id(1)
    heads, dim, rows = q_ref.shape

    @pl.when(block == 0)
    def _():
        for h in range(heads):
            keys[h] = k_ref[h].T
            values[h] = v_ref[h].T
        key_grad[...] = jnp.zeros_like(key_grad)
        value_grad[...] = jnp.zeros_like(value_grad)

    labels = qlab_ref[...]
    queries = [q_ref[h] for h in range(heads)]
    grads = [grad_ref[h] for h in range(heads)]
    query_rows = [q.T for q in queries]
    grad_rows = [g.T for g in grads]
    levels = [lse_ref[h] for h in range(heads)]
    corrections = [
        jnp.sum(
            grads[h].astype(jnp.float32) * out_ref[h].astype(jnp.float32), axis=0, keepdims=True
        )
        for h in range(heads)
    ]

    def step(j, carry):
        start = pl.multiple_of(j * part, part)
        span = pl.ds(start, part)
        same = klab_ref[span, :] == labels
        state = []
        for h in range(heads):
            raw = product(keys[h, span, :], queries[h], ((1,), (0,)))
            grad_prob = product(values[h, span, :], grads[h], ((1,), (0,)))
            prob = jnp.exp2(jnp.where(same, raw * FACTOR - levels[h], MASKED))
            grad_score = (prob * (grad_prob - corrections[h])).astype(jnp.bfloat16)
            value_grad[h, span, :] += product(
                prob.astype(jnp.bfloat16), grad_rows[h], ((1,), (0,))
            )
            key_grad[h, span, :] += product(grad_score, query_rows[h], ((1,), (0,)))
            state.append(carry[h] + product(k_ref[h, :, span], grad_score, ((1,), (0,))))
        return tuple(state)

    empty = tuple(jnp.zeros((dim, rows), jnp.float32) for _ in range(heads))
    result = lax.fori_loop(first_ref[block], last_ref[block], step, empty)
    for h in range(heads):
        dq_ref[h] = result[h] * HEAD_DIM**-0.5

    @pl.when(block == pl.num_programs(1) - 1)
    def _():
        for h in range(heads):
            dk_ref[h] = key_grad[h].T * HEAD_DIM**-0.5
            dv_ref[h] = value_grad[h].T


def split_rows(heads, dim, rows):
    return pl.BlockSpec((heads, dim, rows), lambda h, i, *_: (h, 0, i))


def all_rows(heads, dim, rows):
    return pl.BlockSpec((heads, dim, rows), lambda h, i, *_: (h, 0, 0))


def layout_of(heads, tokens):
    together = 2 if heads % 2 == 0 else 1
    rows = min(tokens, 512)
    part = min(tokens, 512)
    return together, rows, part


def attend(query, keys, values, row_labels, column_labels, first, last):
    heads, dim, tokens = query.shape
    length = keys.shape[2]
    together, rows, part = layout_of(heads, tokens)
    cost = heads * tokens * length
    return pl.pallas_call(
        functools.partial(attend_kernel, part=part),
        grid_spec=pltpu.PrefetchScalarGridSpec(
            num_scalar_prefetch=2,
            grid=(heads // together, tokens // rows),
            in_specs=[
                split_rows(together, dim, rows),
                all_rows(together, dim, length),
                all_rows(together, dim, length),
                pl.BlockSpec((1, rows), lambda h, i, *_: (0, i)),
                pl.BlockSpec((length, 1), lambda h, i, *_: (0, 0)),
            ],
            out_specs=[split_rows(together, dim, rows), split_rows(together, 1, rows)],
            scratch_shapes=[pltpu.VMEM((together, length, dim), jnp.bfloat16)],
        ),
        out_shape=[
            jax.ShapeDtypeStruct((heads, dim, tokens), jnp.bfloat16),
            jax.ShapeDtypeStruct((heads, 1, tokens), jnp.float32),
        ],
        compiler_params=pltpu.CompilerParams(vmem_limit_bytes=VMEM_BYTES),
        cost_estimate=pl.CostEstimate(
            flops=16 * dim * cost // 2, bytes_accessed=8 * heads * dim * length, transcendentals=cost
        ),
    )(first, last, query, keys, values, row_labels, column_labels)


def attend_back(
    query, keys, values, mixture, grad, level, row_labels, column_labels, first, last
):
    heads, dim, tokens = query.shape
    length = keys.shape[2]
    together, rows, part = layout_of(heads, tokens)
    cost = heads * tokens * length
    return pl.pallas_call(
        functools.partial(attend_back_kernel, part=part),
        grid_spec=pltpu.PrefetchScalarGridSpec(
            num_scalar_prefetch=2,
            grid=(heads // together, tokens // rows),
            in_specs=[
                split_rows(together, dim, rows),
                all_rows(together, dim, length),
                all_rows(together, dim, length),
                split_rows(together, dim, rows),
                split_rows(together, dim, rows),
                split_rows(together, 1, rows),
                pl.BlockSpec((1, rows), lambda h, i, *_: (0, i)),
                pl.BlockSpec((length, 1), lambda h, i, *_: (0, 0)),
            ],
            out_specs=[
                split_rows(together, dim, rows),
                all_rows(together, dim, length),
                all_rows(together, dim, length),
            ],
            scratch_shapes=[
                pltpu.VMEM((together, length, dim), jnp.bfloat16),
                pltpu.VMEM((together, length, dim), jnp.bfloat16),
                pltpu.VMEM((together, length, dim), jnp.float32),
                pltpu.VMEM((together, length, dim), jnp.float32),
            ],
        ),
        out_shape=[
            jax.ShapeDtypeStruct((heads, dim, tokens), jnp.float32),
            jax.ShapeDtypeStruct((heads, dim, length), jnp.float32),
            jax.ShapeDtypeStruct((heads, dim, length), jnp.float32),
        ],
        compiler_params=pltpu.CompilerParams(vmem_limit_bytes=VMEM_BYTES),
        cost_estimate=pl.CostEstimate(
            flops=40 * dim * cost // 2,
            bytes_accessed=16 * heads * dim * length,
            transcendentals=cost,
        ),
    )(first, last, query, keys, values, mixture, grad, level, row_labels, column_labels)


def norm_back(grad_full, normal, inverse, gain):
    scaled = grad_full * gain
    mean_grad = jnp.mean(scaled, axis=-1, keepdims=True)
    mean_cross = jnp.mean(scaled * normal, axis=-1, keepdims=True)
    back = inverse * (scaled - mean_grad - normal * mean_cross)
    return (back, jnp.sum(grad_full * normal, axis=0))


def product_of(pattern, left, right):
    return jnp.einsum(pattern, left, right, preferred_element_type=jnp.float32)


def crossed(block):
    return lax.all_to_all(block, "tensor", split_axis=0, concat_axis=0, tiled=True)


def in_order(foremost, own, other):
    return (jnp.where(foremost, own, other), jnp.where(foremost, other, own))


def to_tokens(block):
    tokens, width = block.shape
    parts = crossed(block.reshape(2, tokens // 2, width))
    return jnp.concatenate([parts[0], parts[1]], axis=1)


def to_features(block):
    width = block.shape[1] // 2
    parts = crossed(jnp.stack([block[:, :width], block[:, width:]]))
    return parts.reshape(-1, width)


def on_device(
    block_in, cotangent, segments, w_qkv, w_attn_out, w_mlp_in, w_mlp_out, gain_attn, gain_mlp
):
    tokens, width = block_in.shape
    mine = tokens // 2
    shard = w_qkv.shape[0]
    features = 2 * width
    place = lax.axis_index("tensor")
    units = w_mlp_in.shape[2]
    headed = w_qkv.shape[2]
    local_heads = headed // HEAD_DIM
    wide, down_at = 2 * units, 2 * units + headed

    foremost = place == 0
    other_in = swapped(block_in, "tensor", 0)
    whole_in = jnp.concatenate(in_order(foremost, block_in, other_in), axis=1)
    first_weights = lax.all_gather(
        jnp.concatenate(
            [w_qkv.reshape(shard, 3 * headed), gain_attn[:, None], gain_mlp[:, None]], axis=1
        ),
        "dp",
        axis=0,
        tiled=True,
    )
    full_qkv = first_weights[:, : 3 * headed].reshape(features, 3, local_heads, HEAD_DIM)
    gain_first = first_weights[:, 3 * headed].astype(jnp.float32)
    gain_second = first_weights[:, 3 * headed + 1].astype(jnp.float32)
    half_weights = lax.all_gather(
        jnp.concatenate([w_mlp_in.reshape(shard, wide), w_attn_out.T, w_mlp_out.T], axis=1),
        "dp",
        axis=0,
        tiled=True,
    )
    other_weights = swapped(half_weights, "tensor", 0)
    both_weights = jnp.stack(in_order(foremost, half_weights, other_weights))
    full_in = both_weights[:, :, :wide]
    full_out = both_weights[:, :, wide:down_at]
    full_down = both_weights[:, :, down_at:]
    cot_tok = to_tokens(cotangent)

    half_index = lax.axis_index("dp") % 2
    normal_one, _ = statistics(whole_in.astype(jnp.float32))
    normed_one = (normal_one * gain_first).astype(jnp.bfloat16)
    projected = product_of("td,dchx->chxt", normed_one, full_qkv)
    cosine, sine = rotation(tokens, half_index * tokens)
    query = turn(projected[0], cosine, sine).astype(jnp.bfloat16)
    key_heads = turn(projected[1], cosine, sine).astype(jnp.bfloat16)
    value_heads = projected[2].astype(jnp.bfloat16)
    other_keys, other_values, other_labels = swapped((key_heads, value_heads, segments), "dp", 0)
    leads = half_index == 0

    def ordered(own, other):
        return jnp.concatenate(
            [jnp.where(leads, own, other), jnp.where(leads, other, own)], axis=-1
        )

    all_keys = ordered(key_heads, other_keys)
    all_values = ordered(value_heads, other_values)
    all_labels = ordered(segments, other_labels)
    _, rows, part = layout_of(local_heads, tokens)
    lows = segments[::rows]
    highs = segments[rows - 1 :: rows]
    below = jnp.sum((all_labels[None, :] < lows[:, None]).astype(jnp.int32), axis=1)
    within = jnp.sum((all_labels[None, :] <= highs[:, None]).astype(jnp.int32), axis=1)
    first = below // part
    last = (within + part - 1) // part
    row_labels = segments[None, :]
    column_labels = all_labels[:, None]

    mixture, level = attend(query, all_keys, all_values, row_labels, column_labels, first, last)
    mixture_halves = mixture.reshape(headed, 2, mine).transpose(1, 0, 2)
    mixture_tok = crossed(mixture_halves)
    x_tok = lax.dynamic_slice_in_dim(whole_in, place * mine, mine, 0).astype(jnp.float32)
    middle = x_tok + product_of("nht,ndh->td", mixture_tok, full_out)
    normal_two, inverse_two = statistics(middle)
    normed_two = (normal_two * gain_second).astype(jnp.bfloat16)
    widened = product_of("td,ndf->ntf", normed_two, full_in)
    gated = widened[:, :, units:]
    activated, gelu_pull = jax.vjp(exact_gelu, widened[:, :, :units])
    hidden = (activated * gated).astype(jnp.bfloat16)
    mlp_out = product_of("ntf,ndf->td", hidden, full_down)
    block_out = to_features((middle + mlp_out).astype(jnp.bfloat16))

    grad_down = product_of("td,ntf->ndf", cot_tok, hidden)
    grad_hidden = product_of("td,ndf->ntf", cot_tok, full_down)
    grad_gelu = gelu_pull(grad_hidden * gated)[0]
    grad_wide = jnp.concatenate([grad_gelu, grad_hidden * activated], axis=2).astype(jnp.bfloat16)
    grad_inner = product_of("td,ntf->ndf", normed_two, grad_wide)
    grad_norm_two = product_of("ntf,ndf->td", grad_wide, full_in)
    back_two, gain_grad_two = norm_back(grad_norm_two, normal_two, inverse_two, gain_second)
    grad_middle = cot_tok.astype(jnp.float32) + back_two
    grad_low = grad_middle.astype(jnp.bfloat16)
    grad_mixture = product_of("td,ndh->nht", grad_low, full_out).astype(jnp.bfloat16)
    grad_heads = crossed(grad_mixture).transpose(1, 0, 2).reshape(local_heads, HEAD_DIM, tokens)
    grad_attn = product_of("td,nht->ndh", grad_low, mixture_tok)
    pieces = [part[n] for n in range(2) for part in (grad_inner, grad_attn, grad_down)]
    stacked = jnp.concatenate([piece.astype(jnp.bfloat16) for piece in pieces], axis=1)
    grad_heads, stacked = lax.optimization_barrier((grad_heads, stacked))
    spread = lax.psum_scatter(stacked, "dp", scatter_dimension=0, tiled=True)
    kept, given = in_order(foremost, spread[:, : down_at + units], spread[:, down_at + units :])
    summed = kept.astype(jnp.float32) + swapped(given, "tensor", 0).astype(jnp.float32)

    query_grad, key_grad, value_grad = attend_back(
        query,
        all_keys,
        all_values,
        mixture,
        grad_heads,
        level,
        row_labels,
        column_labels,
        first,
        last,
    )

    def own_sum(both):
        early, late = both[:, :, :tokens], both[:, :, tokens:]
        away = jnp.where(leads, late, early).astype(jnp.bfloat16)
        return jnp.where(leads, early, late) + swapped(away, "dp", 0).astype(jnp.float32)

    grad_query = unturn(query_grad, cosine, sine)
    grad_key = unturn(own_sum(key_grad), cosine, sine)
    grad_proj = jnp.stack([grad_query, grad_key, own_sum(value_grad)]).astype(jnp.bfloat16)
    grad_norm_part = product_of("chxt,dchx->td", grad_proj, full_qkv).astype(jnp.bfloat16)
    kept_norm, given_norm = in_order(foremost, grad_norm_part[:mine], grad_norm_part[mine:])
    grad_norm_one = kept_norm.astype(jnp.float32) + swapped(given_norm, "tensor", 0).astype(
        jnp.float32
    )
    gain_part = jnp.sum(grad_norm_part.astype(jnp.float32) * normal_one, axis=0)
    grad_project = product_of("td,chxt->dchx", normed_one, grad_proj)
    last_grads = jnp.concatenate(
        [
            grad_project.reshape(features, 3 * headed).astype(jnp.bfloat16),
            gain_part[:, None].astype(jnp.bfloat16),
            gain_grad_two[:, None].astype(jnp.bfloat16),
        ],
        axis=1,
    )
    last_sums = lax.psum_scatter(last_grads, "dp", scatter_dimension=0, tiled=True).astype(
        jnp.float32
    )
    summed_qkv = last_sums[:, : 3 * headed]
    gain_halves = last_sums[:, 3 * headed :].T
    gain_sums = lax.dynamic_slice_in_dim(
        gain_halves + swapped(gain_halves, "tensor", 0), place * (shard // 2), shard // 2, 1
    )
    normal_tok, inverse_tok = statistics(x_tok)
    back_one, _ = norm_back(grad_norm_one, normal_tok, inverse_tok, gain_first)
    grad_in = to_features((grad_middle + back_one).astype(jnp.bfloat16))
    return (
        block_out,
        grad_in,
        summed_qkv.reshape(shard, 3, headed),
        summed[:, wide:down_at].T,
        summed[:, :wide].reshape(shard, 2, units),
        summed[:, down_at:].T,
        gain_sums[0],
        gain_sums[1],
    )


def solution(mesh):
    placed = (
        P("dp", "tensor"),
        P("dp", "tensor"),
        P("dp"),
        P("dp", None, "tensor"),
        P("tensor", "dp"),
        P("dp", None, "tensor"),
        P("tensor", "dp"),
        P("dp"),
        P("dp"),
    )
    return jax.shard_map(
        on_device,
        mesh=mesh,
        in_specs=placed,
        out_specs=(
            P("dp", "tensor"),
            P("dp", "tensor"),
            P("dp", None, "tensor"),
            P("tensor", "dp"),
            P("dp", None, "tensor"),
            P("tensor", "dp"),
            P(("dp", "tensor")),
            P(("dp", "tensor")),
        ),
        check_vma=False,
    )
```

profile of v0, /device:TPU:0, one launch (start us, length us, event | category | flops | bytes accessed | tf_op | source)
XLA Modules:
  0.0 673.2 jit_solution(16523013980592046474)
XLA Ops:
  17.9 31.8 %collective-permute-done = bf16[2048,384]{0,1:T(8,128)(2,1)} collective-permute-done((bf16[2048,384]{0,1:T(8,128)(2,1)S(1)}, bf16[2048,384]{0,1:T(8,128)(2,1)}, u32[]{:S(2)}, u32[]{:S(2)}) %collective-permute-start) | collective-permute-done | bytes 1572896 | tf_op jit(solution)/shard_map/ppermute | solution.py:27
  57.1 3.9 copy.149
  62.9 5.5 fusion.53
  78.2 4.8 all-to-all-start.2
  87.1 15.9 %all-to-all-done.2 = bf16[2,1024,384]{1,2,0:T(8,128)(2,1)} async-done(((bf16[2,1024,384]{1,2,0:T(8,128)(2,1)}), bf16[2,1024,384]{1,2,0:T(8,128)(2,1)}, u32[]{:S(2)}, u32[]{:S(2)}) %all-to-all-start.2) | async-done | bytes 1572896 | tf_op jit(solution)/shard_map/all_to_all | solution.py:299
  109.1 4.8 broadcast_select_fusion.3
  113.9 5.4 copy.153
  119.6 3.9 pad_maximum_fusion.5.v_ref
  125.4 109.9 %shard_map.152 = (bf16[6,64,2048]{2,1,0:T(8,128)(2,1)}, f32[6,1,2048]{2,1,0:T(1,128)}) custom-call(s32[4]{0:T(128)} %get-tuple-element.121.first_ref, s32[4]{0:T(128)} %get-tuple-element.120.last_ref, bf16[6,64,2048]{2,1,0:T(8,128)(2,1)} %pad_maximum_fusion.13.q_ref, bf16[6,64,4096]{2,1,0:T(8,128)(2,1)} %pad_maximum_fusion.4.k_ref, ...), custom_call_target="tpu_custom_call" | custom-call | flops 25769803776 | bytes 12582912 | tf_op jit(solution)/shard_map/pallas_call | solution.py:212
  239.8 4.6 all-to-all-start
  244.4 5.4 copy.154
  249.8 3.6 select_bitcast_fusion.1
  257.0 3.8 fusion.74
  261.2 4.1 convolution_bitcast_fusion
  265.3 15.6 %add_convert_fusion = (bf16[2,1024,576]{1,2,0:T(8,128)(2,1)}, f32[2,1024,576]{1,2,0:T(8,128)S(1)}, f32[2,576,1024]{2,1,0:T(8,128)S(1)}) fusion(f32[2,1024,1152]{1,2,0:T(8,128)S(1)} %convolution_bitcast_fusion, bf16[2,768,576]{2,1,0:T(8,128)(2,1)} %pad_maximum_fusion.8, bf16[1024,384]{0,1:T(8,128)(2,1)S(1)} %copy-done.22, bf16[1024,384]{0,1:T(8,128)(2,1)S(1)} %copy-done.21), kind=kOutput, calls=%fused_computation.21 | convolution fusion | flops 1901199360 | bytes 24576000 | tf_op jit(solution)/shard_map/td,ndf->ntf/dot_general | solution.py:295
  280.9 4.0 fusion.8
  284.9 6.9 %fusion.27 = (bf16[768]{0:T(1024)(128)(2,1)S(1)}, f32[1024]{0:T(1024)S(1)}, f32[1024]{0:T(1024)S(1)}, f32[1024,768,1]{0,1,2:T(8,128)S(1)}) fusion(f32[1024,768]{0,1:T(8,128)S(1)} %get-tuple-element.115, f32[1024]{0:T(1024)S(1)} %add_rsqrt_fusion.2, f32[1024]{0:T(1024)S(1)} %broadcast_multiply_fusion.6, f32[768]{0:T(1024)S(1)} %get-tuple-element.67, ...), kind=kOutput, calls=%fused_computation.64 | convolution fusion | flops 3646682368 | bytes 17519104 | tf_op jit(solution)/shard_map/ntf,ndf->td/dot_general | solution.py:295
  291.9 6.0 fusion.15
  308.5 4.7 all-to-all-start.3
  321.3 4.1 all-to-all-done.3
  331.1 146.3 %shard_map.153 = (f32[6,64,2048]{2,1,0:T(8,128)}, f32[6,64,4096]{2,1,0:T(8,128)}, f32[6,64,4096]{2,1,0:T(8,128)}) custom-call(s32[4]{0:T(128)} %get-tuple-element.121.first_ref, s32[4]{0:T(128)} %get-tuple-element.120.last_ref, bf16[6,64,2048]{2,1,0:T(8,128)(2,1)} %pad_maximum_fusion.13.q_ref, bf16[6,64,4096]{2,1,0:T(8,128)(2,1)} %pad_maximum_fusion.4.k_ref, ...), custom_call_target="tpu_custom_call" | custom-call | flops 64424509440 | bytes 25165824 | tf_op jit(solution)/shard_map/pallas_call | solution.py:245
  490.0 4.1 fusion.35
  494.1 6.7 fusion.5
  506.8 9.4 %copy.209 = bf16[768,4224]{1,0:T(8,128)(2,1)} copy(bf16[768,4224]{0,1:T(8,128)(2,1)} %fusion.55) | data formatting | bytes 12976128
  521.0 3.9 fusion.28
  526.3 3.7 all-to-all-start.1
  530.0 27.2 %collective-permute-done.7 = bf16[1024,768]{0,1:T(8,128)(2,1)} collective-permute-done((bf16[1024,768]{0,1:T(8,128)(2,1)}, bf16[1024,768]{0,1:T(8,128)(2,1)}, u32[]{:S(2)}, u32[]{:S(2)}) %collective-permute-start.7) | collective-permute-done | bytes 1572896 | tf_op jit(solution)/shard_map/ppermute | solution.py:27
  565.2 8.3 %all-to-all-done.1 = bf16[2,1024,384]{1,2,0:T(8,128)(2,1)S(1)} async-done(((bf16[2,1024,384]{1,2,0:T(8,128)(2,1)}), bf16[2,1024,384]{1,2,0:T(8,128)(2,1)S(1)}, u32[]{:S(2)}, u32[]{:S(2)}) %all-to-all-start.1) | async-done | bytes 1572896 | tf_op jit(solution)/shard_map/all_to_all | solution.py:299
  573.5 3.8 all-to-all-start.4
  582.9 13.6 %all-to-all-done.4 = bf16[2,1024,384]{1,2,0:T(8,128)(2,1)S(1)} async-done(((bf16[2,1024,384]{1,2,0:T(8,128)(2,1)}), bf16[2,1024,384]{1,2,0:T(8,128)(2,1)S(1)}, u32[]{:S(2)}, u32[]{:S(2)}) %all-to-all-start.4) | async-done | bytes 1572896 | tf_op jit(solution)/shard_map/all_to_all | solution.py:299
  599.7 54.4 %reduce-scatter.9.cloned.1.call-done = bf16[48,4224]{1,0:T(8,128)(2,1)} async-done(((bf16[768,4224]{1,0:T(8,128)(2,1)}), bf16[48,4224]{1,0:T(8,128)(2,1)}) %reduce-scatter.9.cloned.1.call-update) | async-done | bytes 405520
  658.4 4.8 collective-permute-done.8
  (230 shorter events, 123.3 us)
Async XLA Ops:
  7.2 8.1 %copy-start.36 = (bf16[48,2,576]{2,1,0:T(2,128)(2,1)S(1)}, bf16[48,2,576]{2,1,0:T(2,128)(2,1)}, u32[]{:S(2)}) copy-start(bf16[48,2,576]{2,1,0:T(2,128)(2,1)} %param.14) | copy-start | bytes 331780
  7.2 8.2 %copy-start.40 = (bf16[384,48]{0,1:T(8,128)(2,1)S(1)}, bf16[384,48]{0,1:T(8,128)(2,1)}, u32[]{:S(2)}) copy-start(bf16[384,48]{0,1:T(8,128)(2,1)} %param.13) | copy-start | bytes 110596
  7.2 8.2 %copy-start.37 = (bf16[576,48]{0,1:T(8,128)(2,1)S(1)}, bf16[576,48]{0,1:T(8,128)(2,1)}, u32[]{:S(2)}) copy-start(bf16[576,48]{0,1:T(8,128)(2,1)} %param.15) | copy-start | bytes 165892
  7.2 47.1 %all-gather.3.cloned.1.call-start = ((), (), s32[]{:S(2)}) async-start(), calls=%async_computation.7 | async-start | bytes 2088960 | tf_op jit(solution)/shard_map/all_gather | solution.py:334
  10.5 103.4 %all-gather.5.cloned.1.call-start = ((), (), s32[]{:S(2)}) async-start(), calls=%async_computation.8 | async-start | bytes 3551232 | tf_op jit(solution)/shard_map/all_gather | solution.py:345
  12.2 37.5 %collective-permute-start = (bf16[2048,384]{0,1:T(8,128)(2,1)S(1)}, bf16[2048,384]{0,1:T(8,128)(2,1)}, u32[]{:S(2)}, u32[]{:S(2)}) collective-permute-start(bf16[2048,384]{0,1:T(8,128)(2,1)S(1)} %copy.144), channel_id=1, source_target_pairs={{0,1},{1,0},{2,3},{3,2},{4,5},{5,4},{6,7},{7,6},{8,9},{9,8},{10,11... | collective-permute-start | bytes 4718600 | tf_op jit(solution)/shard_map/ppermute | solution.py:27
  17.9 51.3 %copy-start.27 = (f32[32,2048]{1,0:T(8,128)}, f32[32,2048]{1,0:T(8,128)S(1)}, u32[]{:S(2)}) copy-start(f32[32,2048]{1,0:T(8,128)S(1)} %get-tuple-element.110) | copy-start | bytes 786436
  51.9 53.8 %copy-start.2 = (bf16[2048,384]{0,1:T(8,128)(2,1)}, bf16[2048,384]{0,1:T(8,128)(2,1)S(1)}, u32[]{:S(2)}) copy-start(bf16[2048,384]{0,1:T(8,128)(2,1)S(1)} %get-tuple-element.94) | copy-start | bytes 4718596
  51.9 53.8 %copy-start.4 = (bf16[2048,384]{0,1:T(8,128)(2,1)}, bf16[2048,384]{0,1:T(8,128)(2,1)S(1)}, u32[]{:S(2)}) copy-start(bf16[2048,384]{0,1:T(8,128)(2,1)S(1)} %get-tuple-element.95) | copy-start | bytes 4718596
  52.4 9.9 %copy-start.41 = (f32[2048]{0:T(1024)}, f32[2048]{0:T(1024)S(1)}, u32[]{:S(2)}) copy-start(f32[2048]{0:T(1024)S(1)} %broadcast_multiply_fusion) | copy-start | bytes 24580
  53.2 9.1 %copy-start.44 = (f32[2048]{0:T(1024)}, f32[2048]{0:T(1024)S(1)}, u32[]{:S(2)}) copy-start(f32[2048]{0:T(1024)S(1)} %add_rsqrt_fusion) | copy-start | bytes 24580
  75.1 34.0 %collective-permute-start.2 = (bf16[6,64,2048]{2,1,0:T(8,128)(2,1)}, bf16[6,64,2048]{2,1,0:T(8,128)(2,1)}, u32[]{:S(2)}, u32[]{:S(2)}) collective-permute-start(bf16[6,64,2048]{2,1,0:T(8,128)(2,1)} %pad_maximum_fusion.14), channel_id=1, source_target_pairs={{0,2},{2,0},{4,6},{6,4},{8,10},{10,8},{12,14},{14,12},{16,18},{18,... | collective-permute-start | bytes 4718600 | tf_op jit(solution)/shard_map/ppermute | solution.py:27
  75.4 33.7 %collective-permute-start.3 = (bf16[6,64,2048]{2,1,0:T(8,128)(2,1)}, bf16[6,64,2048]{2,1,0:T(8,128)(2,1)}, u32[]{:S(2)}, u32[]{:S(2)}) collective-permute-start(bf16[6,64,2048]{2,1,0:T(8,128)(2,1)} %fusion.38), channel_id=1, source_target_pairs={{0,2},{2,0},{4,6},{6,4},{8,10},{10,8},{12,14},{14,12},{16,18},{18,... | collective-permute-start | bytes 4718600 | tf_op jit(solution)/shard_map/ppermute | solution.py:27
  75.6 7.4 %copy-start.46 = (s32[2048]{0:T(1024)S(1)}, s32[2048]{0:T(1024)}, u32[]{:S(2)}) copy-start(s32[2048]{0:T(1024)} %param.11) | copy-start | bytes 24580
  78.2 24.8 %all-to-all-start.2 = ((bf16[2,1024,384]{1,2,0:T(8,128)(2,1)}), bf16[2,1024,384]{1,2,0:T(8,128)(2,1)}, u32[]{:S(2)}, u32[]{:S(2)}) async-start(bf16[2,1024,384]{1,2,0:T(8,128)(2,1)} %copy.161), calls=%async_computation.2 | async-start | bytes 3145728 | tf_op jit(solution)/shard_map/all_to_all | solution.py:299
  83.0 1.2 collective-permute-start.1
  119.3 125.1 %collective-permute-start.4 = (bf16[768,2112]{0,1:T(8,128)(2,1)}, bf16[768,2112]{0,1:T(8,128)(2,1)}, u32[]{:S(2)}, u32[]{:S(2)}) collective-permute-start(bf16[768,2112]{0,1:T(8,128)(2,1)} %copy.153), channel_id=1, source_target_pairs={{0,1},{1,0},{2,3},{3,2},{4,5},{5,4},{6,7},{7,6},{8,9},{9,8},{10,11... | collective-permute-start | bytes 9732104 | tf_op jit(solution)/shard_map/ppermute | solution.py:27
  239.8 17.2 %all-to-all-start = ((bf16[2,384,1024]{2,1,0:T(8,128)(2,1)}), bf16[2,384,1024]{2,1,0:T(8,128)(2,1)}, u32[]{:S(2)}, u32[]{:S(2)}) async-start(bf16[2,384,1024]{2,1,0:T(8,128)(2,1)} %bitcast.160), calls=%async_computation | async-start | bytes 3145728 | tf_op jit(solution)/shard_map/all_to_all | solution.py:299
  260.8 43.8 %copy-start.8 = (f32[1024,768]{0,1:T(8,128)}, f32[1024,768]{0,1:T(8,128)S(1)}, u32[]{:S(2)}) copy-start(f32[1024,768]{0,1:T(8,128)S(1)} %get-tuple-element.115) | copy-start | bytes 9437188
  305.8 7.4 %copy-start.10 = (f32[1024,768]{0,1:T(8,128)}, f32[1024,768]{0,1:T(8,128)S(1)}, u32[]{:S(2)}) copy-start(f32[1024,768]{0,1:T(8,128)S(1)} %multiply_add_fusion) | copy-start | bytes 9437188
  308.5 16.9 %all-to-all-start.3 = ((bf16[2,384,1024]{2,1,0:T(8,128)(2,1)}), bf16[2,384,1024]{2,1,0:T(8,128)(2,1)}, u32[]{:S(2)}, u32[]{:S(2)}) async-start(bf16[2,384,1024]{2,1,0:T(8,128)(2,1)} %convolution_convert_fusion.1), calls=%async_computation.3 | async-start | bytes 3145728 | tf_op jit(solution)/shard_map/all_to_all | solution.py:299
  313.1 264.2 %reduce-scatter.7.cloned.1.call-start = ((), (), s32[]{:S(2)}) async-start(), calls=%async_computation.9 | async-start | bytes 2088960
  477.4 7.7 %copy-start.7 = (f32[6,64,4096]{2,1,0:T(8,128)S(1)}, f32[6,64,4096]{2,1,0:T(8,128)}, u32[]{:S(2)}) copy-start(f32[6,64,4096]{2,1,0:T(8,128)} %get-tuple-element.19) | copy-start | bytes 18874372
  480.7 4.4 collective-permute-start.5
  484.5 3.6 collective-permute-start.6
  506.7 147.4 %reduce-scatter.9.cloned.1.call-start = ((), (), s32[]{:S(2)}) async-start(), calls=%async_computation.10 | async-start | bytes 6893568
  519.7 37.5 %collective-permute-start.7 = (bf16[1024,768]{0,1:T(8,128)(2,1)}, bf16[1024,768]{0,1:T(8,128)(2,1)}, u32[]{:S(2)}, u32[]{:S(2)}) collective-permute-start(bf16[1024,768]{0,1:T(8,128)(2,1)} %broadcast_select_fusion), channel_id=1, source_target_pairs={{0,1},{1,0},{2,3},{3,2},{4,5},{5,4},{6,7},{7,6},{8,9},{9,8},{10,11... | collective-permute-start | bytes 4718600 | tf_op jit(solution)/shard_map/ppermute | solution.py:27
  526.3 47.2 %all-to-all-start.1 = ((bf16[2,1024,384]{1,2,0:T(8,128)(2,1)}), bf16[2,1024,384]{1,2,0:T(8,128)(2,1)S(1)}, u32[]{:S(2)}, u32[]{:S(2)}) async-start(bf16[2,1024,384]{1,2,0:T(8,128)(2,1)} %pad_maximum_fusion.15), calls=%async_computation.1 | async-start | bytes 3145728 | tf_op jit(solution)/shard_map/all_to_all | solution.py:299
  530.0 30.8 %copy-start.11 = (f32[1024,768]{0,1:T(8,128)S(1)}, f32[1024,768]{0,1:T(8,128)}, u32[]{:S(2)}) copy-start(f32[1024,768]{0,1:T(8,128)} %copy-done.10) | copy-start | bytes 9437188
  573.5 23.0 %all-to-all-start.4 = ((bf16[2,1024,384]{1,2,0:T(8,128)(2,1)}), bf16[2,1024,384]{1,2,0:T(8,128)(2,1)S(1)}, u32[]{:S(2)}, u32[]{:S(2)}) async-start(bf16[2,1024,384]{1,2,0:T(8,128)(2,1)} %pad_maximum_fusion.17), calls=%async_computation.4 | async-start | bytes 3145728 | tf_op jit(solution)/shard_map/all_to_all | solution.py:299
  579.3 19.7 %collective-permute-start.9 = (f32[2,48]{1,0:T(2,128)S(1)}, f32[2,48]{1,0:T(2,128)S(1)}, u32[]{:S(2)}, u32[]{:S(2)}) collective-permute-start(f32[2,48]{1,0:T(2,128)S(1)} %slice_bitcast_fusion.16), channel_id=1, source_target_pairs={{0,1},{1,0},{2,3},{3,2},{4,5},{5,4},{6,7},{7,6},{8,9},{9,8},{10,11... | collective-permute-start | bytes 1160 | tf_op jit(solution)/shard_map/ppermute | solution.py:27
  656.3 6.8 %collective-permute-start.8 = (bf16[48,2112]{1,0:T(8,128)(2,1)S(1)}, bf16[48,2112]{1,0:T(8,128)(2,1)S(1)}, u32[]{:S(2)}, u32[]{:S(2)}) collective-permute-start(bf16[48,2112]{1,0:T(8,128)(2,1)S(1)} %copy.175), channel_id=1, source_target_pairs={{0,1},{1,0},{2,3},{3,2},{4,5},{5,4},{6,7},{7,6},{8,9},{9,8},{10,11... | collective-permute-start | bytes 608264 | tf_op jit(solution)/shard_map/ppermute | solution.py:27
  (37 other events, 119.6 us)
Sparse Core Ops, SparseCore 0:
  10.9 43.3 all-gather.2
  57.1 45.2 all-gather.4
  506.9 57.2 reduce-scatter.6
  568.0 86.1 reduce-scatter.8
where the time goes:
time: 682 us; the launch traced here: 673 us
  Pallas kernels  256 us (38%)
  waiting for transfers between devices  162 us (24%)
  local copies, waits for them, and re-layouts  82.7 us (12%)
  matrix products  65.4 us (10%)
  other arithmetic  61.5 us (9%)
  starting transfers between devices  30 us (4%)
  between operations  15.1 us (2%)
    pallas_call x1, Pallas kernels, attend_back(): pl.pallas_call(functools.partial(attend_back_kernel, part=part), grid_spe...  146 us
    pallas_call x1, Pallas kernels, attend(): pl.pallas_call(functools.partial(attend_kernel, part=part), grid_spec=plt...  110 us
    dot_general x12, matrix products, product_of(): return jnp.einsum(pattern, left, right, preferred_element_type=jnp.float32)  65.4 us
    ppermute x10, waiting for transfers between devices, swapped(): return lax.ppermute(block, axis, route)  64.7 us
    unnamed x6, waiting for transfers between devices  54.5 us
    all_to_all x5, waiting for transfers between devices, crossed(): lax.all_to_all(block, 'tensor', split_axis=0, concat_axis=0, tiled=True)  41.9 us
    unnamed x115, local copies, waits for them, and re-layouts  31.2 us
    all_to_all x5, starting transfers between devices, crossed(): lax.all_to_all(block, 'tensor', split_axis=0, concat_axis=0, tiled=True)  21.5 us
  transfers between devices with their start and end apart: 19, of which 11 were waited for; matrix products, arithmetic and copies ran while one was open for 17% of the time, Pallas kernels for 16%

commit v1 on v0

--- a/solution.py
+++ b/solution.py
@@ -410,12 +410,15 @@
     grad_mixture = product_of("td,ndh->nht", grad_low, full_out).astype(jnp.bfloat16)
     grad_heads = crossed(grad_mixture).transpose(1, 0, 2).reshape(local_heads, HEAD_DIM, tokens)
     grad_attn = product_of("td,nht->ndh", grad_low, mixture_tok)
-    pieces = [part[n] for n in range(2) for part in (grad_inner, grad_attn, grad_down)]
-    stacked = jnp.concatenate([piece.astype(jnp.bfloat16) for piece in pieces], axis=1)
-    grad_heads, stacked = lax.optimization_barrier((grad_heads, stacked))
-    spread = lax.psum_scatter(stacked, "dp", scatter_dimension=0, tiled=True)
-    kept, given = in_order(foremost, spread[:, : down_at + units], spread[:, down_at + units :])
-    summed = kept.astype(jnp.float32) + swapped(given, "tensor", 0).astype(jnp.float32)
+    halves = [
+        jnp.concatenate([grad_inner[n], grad_attn[n], grad_down[n]], axis=1).astype(jnp.bfloat16)
+        for n in range(2)
+    ]
+    kept, given = in_order(foremost, halves[0], halves[1])
+    grad_heads, kept, given = lax.optimization_barrier((grad_heads, kept, given))
+    received = swapped(given, "tensor", 0)
+    halved = (kept.astype(jnp.float32) + received.astype(jnp.float32)).astype(jnp.bfloat16)
+    summed = lax.psum_scatter(halved, "dp", scatter_dimension=0, tiled=True).astype(jnp.float32)
 
     query_grad, key_grad, value_grad = attend_back(
         query,

time: 682 us -> 663 us (0.972); the launches traced: 673 us -> 672 us
  Pallas kernels: 256 us -> 224 us
  starting transfers between devices: 30 us -> 61 us
  other arithmetic: 61.5 us -> 78.9 us
  waiting for transfers between devices: 162 us -> 145 us
    unnamed x6 -> x5, waiting for transfers between devices: 54.5 us -> 0.09 us
    ppermute x10, starting transfers between devices: 8.33 us -> 39.3 us  [swapped(): return lax.ppermute(block, axis, route)]
    pallas_call x1, Pallas kernels: 146 us -> 128 us  [attend_back(): pl.pallas_call(functools.partial(attend_back_kernel, part=part), grid_spe...]
    unnamed x115 -> x98, local copies, waits for them, and re-layouts: 31.2 us -> 13.5 us
    ppermute x10, waiting for transfers between devices: 64.7 us -> 82 us  [swapped(): return lax.ppermute(block, axis, route)]
    reduce_scatter x0 -> x1, waiting for transfers between devices: none -> 17.2 us  [on_device(): lax.psum_scatter(halved, 'dp', scatter_dimension=0, tiled=True)]
    pallas_call x1, Pallas kernels: 110 us -> 95.3 us  [attend(): pl.pallas_call(functools.partial(attend_kernel, part=part), grid_spec=plt...]
  transfers between devices with their start and end apart: 19 -> 19, of which waited for: 11 -> 10; matrix products, arithmetic and copies ran while one was open for 17% -> 21% of each run, Pallas kernels for 16% -> 14%
where the time goes in v1:
time: 663 us; the launch traced here: 672 us
  Pallas kernels  224 us (34%)
  waiting for transfers between devices  145 us (22%)
  local copies, waits for them, and re-layouts  86.3 us (13%)
  other arithmetic  78.9 us (12%)
  matrix products  61.8 us (9%)
  starting transfers between devices  61 us (9%)
  between operations  14.9 us (2%)
    pallas_call x1, Pallas kernels, attend_back(): pl.pallas_call(functools.partial(attend_back_kernel, part=part), grid_spe...  128 us
    pallas_call x1, Pallas kernels, attend(): pl.pallas_call(functools.partial(attend_kernel, part=part), grid_spec=plt...  95.3 us
    ppermute x10, waiting for transfers between devices, swapped(): return lax.ppermute(block, axis, route)  82 us
    dot_general x12, matrix products, product_of(): return jnp.einsum(pattern, left, right, preferred_element_type=jnp.float32)  61.8 us
    all_to_all x5, waiting for transfers between devices, crossed(): lax.all_to_all(block, 'tensor', split_axis=0, concat_axis=0, tiled=True)  45.2 us
    ppermute x10, starting transfers between devices, swapped(): return lax.ppermute(block, axis, route)  39.3 us
    all_to_all x5, starting transfers between devices, crossed(): lax.all_to_all(block, 'tensor', split_axis=0, concat_axis=0, tiled=True)  21.6 us
    reduce_scatter x1, waiting for transfers between devices, on_device(): lax.psum_scatter(halved, 'dp', scatter_dimension=0, tiled=True)  17.2 us
  transfers between devices with their start and end apart: 19, of which 10 were waited for; matrix products, arithmetic and copies ran while one was open for 21% of the time, Pallas kernels for 14%

profile of v1, /device:TPU:0, one launch (start us, length us, event | category | flops | bytes accessed | tf_op | source)
XLA Modules:
  0.0 672.1 jit_solution(16462902517289838511)
XLA Ops:
  17.9 31.8 %collective-permute-done = bf16[2048,384]{0,1:T(8,128)(2,1)} collective-permute-done((bf16[2048,384]{0,1:T(8,128)(2,1)S(1)}, bf16[2048,384]{0,1:T(8,128)(2,1)}, u32[]{:S(2)}, u32[]{:S(2)}) %collective-permute-start) | collective-permute-done | bytes 1572896 | tf_op jit(solution)/shard_map/ppermute | solution.py:27
  62.9 5.5 fusion.51
  78.3 4.8 all-to-all-start.2
  87.1 16.0 %all-to-all-done.2 = bf16[2,1024,384]{1,2,0:T(8,128)(2,1)} async-done(((bf16[2,1024,384]{1,2,0:T(8,128)(2,1)}), bf16[2,1024,384]{1,2,0:T(8,128)(2,1)}, u32[]{:S(2)}, u32[]{:S(2)}) %all-to-all-start.2) | async-done | bytes 1572896 | tf_op jit(solution)/shard_map/all_to_all | solution.py:299
  109.1 4.8 broadcast_select_fusion.5
  113.9 5.4 copy.191
  125.4 95.3 %shard_map.152 = (bf16[6,64,2048]{2,1,0:T(8,128)(2,1)}, f32[6,1,2048]{2,1,0:T(1,128)}) custom-call(s32[4]{0:T(128)} %get-tuple-element.129.first_ref, s32[4]{0:T(128)} %get-tuple-element.128.last_ref, bf16[6,64,2048]{2,1,0:T(8,128)(2,1)} %pad_maximum_fusion.15.q_ref, bf16[6,64,4096]{2,1,0:T(8,128)(2,1)} %pad_maximum_fusion.6.k_ref, ...), custom_call_target="tpu_custom_call" | custom-call | flops 25769803776 | bytes 12582912 | tf_op jit(solution)/shard_map/pallas_call | solution.py:212
  225.2 4.8 all-to-all-start
  230.0 5.4 copy.192
  250.8 14.7 %add_convert_fusion.1 = (bf16[2,1024,576]{1,2,0:T(8,128)(2,1)}, f32[2,1024,576]{1,2,0:T(8,128)S(1)}, f32[2,576,1024]{2,1,0:T(8,128)}) fusion(f32[2,1024,1152]{1,2,0:T(8,128)S(1)} %convolution_bitcast_fusion, bf16[2,768,576]{2,1,0:T(8,128)(2,1)S(1)} %copy-done.28, bf16[1024,384]{0,1:T(8,128)(2,1)S(1)} %copy-done.19, bf16[1024,384]{0,1:T(8,128)(2,1)S(1)} %copy-done.18), kind=kOutput, calls=%fused_computation.22 | convolution fusion | flops 1901199360 | bytes 24576000 | tf_op jit(solution)/shard_map/td,ndf->ntf/dot_general | solution.py:295
  265.5 6.0 fusion.8
  271.5 6.5 fusion.15
  297.3 4.6 all-to-all-start.3
  302.0 4.7 broadcast_select_fusion
  306.7 7.5 %all-to-all-done.3 = bf16[2,384,1024]{2,1,0:T(8,128)(2,1)} async-done(((bf16[2,384,1024]{2,1,0:T(8,128)(2,1)}), bf16[2,384,1024]{2,1,0:T(8,128)(2,1)}, u32[]{:S(2)}, u32[]{:S(2)}) %all-to-all-start.3) | async-done | bytes 1572896 | tf_op jit(solution)/shard_map/all_to_all | solution.py:299
  314.2 4.2 copy.205
  322.3 128.3 %shard_map.153 = (f32[6,64,2048]{2,1,0:T(8,128)}, f32[6,64,4096]{2,1,0:T(8,128)}, f32[6,64,4096]{2,1,0:T(8,128)}) custom-call(s32[4]{0:T(128)} %get-tuple-element.129.first_ref, s32[4]{0:T(128)} %get-tuple-element.128.last_ref, bf16[6,64,2048]{2,1,0:T(8,128)(2,1)} %pad_maximum_fusion.15.q_ref, bf16[6,64,4096]{2,1,0:T(8,128)(2,1)} %pad_maximum_fusion.6.k_ref, ...), custom_call_target="tpu_custom_call" | custom-call | flops 64424509440 | bytes 25165824 | tf_op jit(solution)/shard_map/pallas_call | solution.py:245
  450.6 4.3 select_convert_fusion.1
  454.8 31.3 %collective-permute-start.5 = (bf16[6,64,2048]{2,1,0:T(8,128)(2,1)}, bf16[6,64,2048]{2,1,0:T(8,128)(2,1)}, u32[]{:S(2)}, u32[]{:S(2)}) collective-permute-start(bf16[6,64,2048]{2,1,0:T(8,128)(2,1)} %select_convert_fusion.1), channel_id=1, source_target_pairs={{0,2},{2,0},{4,6},{6,4},{8,10},{10,8},{12,14},{14,12},{16,18},{18,... | collective-permute-start | bytes 4718600 | tf_op jit(solution)/shard_map/ppermute | solution.py:27
  486.1 4.3 select_convert_fusion
  494.1 4.3 convert_add_fusion.1
  504.1 5.5 fusion.5
  509.7 5.3 fusion.33
  514.9 9.0 %concatenate.66 = bf16[768,1154]{0,1:T(8,128)(2,1)} concatenate(bf16[768,1152]{0,1:T(8,128)(2,1)} %bitcast.152, bf16[768,1]{0,1:T(2,128)(2,1)S(1)} %convert_element_type.175, bf16[768,1]{0,1:T(2,128)(2,1)S(1)} %convert_element_type.177), dimensions={1} | concatenate | bytes 3545088 | tf_op jit(solution)/shard_map/concatenate | solution.py:451
  530.8 36.3 %collective-permute-done.8 = bf16[768,2112]{0,1:T(8,128)(2,1)} collective-permute-done((bf16[768,2112]{0,1:T(8,128)(2,1)}, bf16[768,2112]{0,1:T(8,128)(2,1)}, u32[]{:S(2)}, u32[]{:S(2)}) %collective-permute-start.8) | collective-permute-done | bytes 3244064 | tf_op jit(solution)/shard_map/ppermute | solution.py:27
  567.2 4.2 copy.218
  571.4 4.5 add_convert_fusion
  577.9 4.8 fusion.28
  587.8 13.0 %collective-permute-done.7 = bf16[1024,768]{0,1:T(8,128)(2,1)} collective-permute-done((bf16[1024,768]{0,1:T(8,128)(2,1)}, bf16[1024,768]{0,1:T(8,128)(2,1)}, u32[]{:S(2)}, u32[]{:S(2)}) %collective-permute-start.7) | collective-permute-done | bytes 1572896 | tf_op jit(solution)/shard_map/ppermute | solution.py:27
  609.3 7.9 %all-to-all-done.1 = bf16[2,1024,384]{1,2,0:T(8,128)(2,1)S(1)} async-done(((bf16[2,1024,384]{1,2,0:T(8,128)(2,1)}), bf16[2,1024,384]{1,2,0:T(8,128)(2,1)S(1)}, u32[]{:S(2)}, u32[]{:S(2)}) %all-to-all-start.1) | async-done | bytes 1572896 | tf_op jit(solution)/shard_map/all_to_all | solution.py:299
  626.5 13.8 %all-to-all-done.4 = bf16[2,1024,384]{1,2,0:T(8,128)(2,1)S(1)} async-done(((bf16[2,1024,384]{1,2,0:T(8,128)(2,1)}), bf16[2,1024,384]{1,2,0:T(8,128)(2,1)S(1)}, u32[]{:S(2)}, u32[]{:S(2)}) %all-to-all-start.4) | async-done | bytes 1572896 | tf_op jit(solution)/shard_map/all_to_all | solution.py:299
  644.1 17.2 %reduce-scatter.5.cloned.1.call-done = bf16[48,2112]{1,0:T(8,128)(2,1)} async-done(((bf16[768,2112]{1,0:T(8,128)(2,1)}), bf16[48,2112]{1,0:T(8,128)(2,1)}) %reduce-scatter.5.cloned.1.call-update) | async-done | bytes 202768 | tf_op jit(solution)/shard_map/reduce_scatter | solution.py:421
  (218 shorter events, 141.3 us)
Async XLA Ops:
  7.2 8.1 %copy-start.33 = (bf16[48,2,576]{2,1,0:T(2,128)(2,1)S(1)}, bf16[48,2,576]{2,1,0:T(2,128)(2,1)}, u32[]{:S(2)}) copy-start(bf16[48,2,576]{2,1,0:T(2,128)(2,1)} %param.14) | copy-start | bytes 331780
  7.2 8.2 %copy-start.37 = (bf16[384,48]{0,1:T(8,128)(2,1)S(1)}, bf16[384,48]{0,1:T(8,128)(2,1)}, u32[]{:S(2)}) copy-start(bf16[384,48]{0,1:T(8,128)(2,1)} %param.13) | copy-start | bytes 110596
  7.2 8.2 %copy-start.34 = (bf16[576,48]{0,1:T(8,128)(2,1)S(1)}, bf16[576,48]{0,1:T(8,128)(2,1)}, u32[]{:S(2)}) copy-start(bf16[576,48]{0,1:T(8,128)(2,1)} %param.15) | copy-start | bytes 165892
  7.2 47.1 %all-gather.3.cloned.1.call-start = ((), (), s32[]{:S(2)}) async-start(), calls=%async_computation.7 | async-start | bytes 2088960 | tf_op jit(solution)/shard_map/all_gather | solution.py:334
  10.5 103.4 %all-gather.5.cloned.1.call-start = ((), (), s32[]{:S(2)}) async-start(), calls=%async_computation.8 | async-start | bytes 3551232 | tf_op jit(solution)/shard_map/all_gather | solution.py:345
  12.2 37.5 %collective-permute-start = (bf16[2048,384]{0,1:T(8,128)(2,1)S(1)}, bf16[2048,384]{0,1:T(8,128)(2,1)}, u32[]{:S(2)}, u32[]{:S(2)}) collective-permute-start(bf16[2048,384]{0,1:T(8,128)(2,1)S(1)} %copy.182), channel_id=1, source_target_pairs={{0,1},{1,0},{2,3},{3,2},{4,5},{5,4},{6,7},{7,6},{8,9},{9,8},{10,11... | collective-permute-start | bytes 4718600 | tf_op jit(solution)/shard_map/ppermute | solution.py:27
  17.9 51.3 %copy-start.24 = (f32[32,2048]{1,0:T(8,128)}, f32[32,2048]{1,0:T(8,128)S(1)}, u32[]{:S(2)}) copy-start(f32[32,2048]{1,0:T(8,128)S(1)} %get-tuple-element.118) | copy-start | bytes 786436
  51.9 53.9 %copy-start.2 = (bf16[2048,384]{0,1:T(8,128)(2,1)}, bf16[2048,384]{0,1:T(8,128)(2,1)S(1)}, u32[]{:S(2)}) copy-start(bf16[2048,384]{0,1:T(8,128)(2,1)S(1)} %get-tuple-element.100) | copy-start | bytes 4718596
  51.9 53.9 %copy-start.4 = (bf16[2048,384]{0,1:T(8,128)(2,1)}, bf16[2048,384]{0,1:T(8,128)(2,1)S(1)}, u32[]{:S(2)}) copy-start(bf16[2048,384]{0,1:T(8,128)(2,1)S(1)} %get-tuple-element.101) | copy-start | bytes 4718596
  52.4 9.9 %copy-start.38 = (f32[2048]{0:T(1024)}, f32[2048]{0:T(1024)S(1)}, u32[]{:S(2)}) copy-start(f32[2048]{0:T(1024)S(1)} %broadcast_multiply_fusion) | copy-start | bytes 24580
  53.2 9.1 %copy-start.41 = (f32[2048]{0:T(1024)}, f32[2048]{0:T(1024)S(1)}, u32[]{:S(2)}) copy-start(f32[2048]{0:T(1024)S(1)} %add_rsqrt_fusion) | copy-start | bytes 24580
  75.2 33.9 %collective-permute-start.2 = (bf16[6,64,2048]{2,1,0:T(8,128)(2,1)}, bf16[6,64,2048]{2,1,0:T(8,128)(2,1)}, u32[]{:S(2)}, u32[]{:S(2)}) collective-permute-start(bf16[6,64,2048]{2,1,0:T(8,128)(2,1)} %pad_maximum_fusion.16), channel_id=1, source_target_pairs={{0,2},{2,0},{4,6},{6,4},{8,10},{10,8},{12,14},{14,12},{16,18},{18,... | collective-permute-start | bytes 4718600 | tf_op jit(solution)/shard_map/ppermute | solution.py:27
  75.5 33.6 %collective-permute-start.3 = (bf16[6,64,2048]{2,1,0:T(8,128)(2,1)}, bf16[6,64,2048]{2,1,0:T(8,128)(2,1)}, u32[]{:S(2)}, u32[]{:S(2)}) collective-permute-start(bf16[6,64,2048]{2,1,0:T(8,128)(2,1)} %fusion.36), channel_id=1, source_target_pairs={{0,2},{2,0},{4,6},{6,4},{8,10},{10,8},{12,14},{14,12},{16,18},{18,... | collective-permute-start | bytes 4718600 | tf_op jit(solution)/shard_map/ppermute | solution.py:27
  75.7 7.4 %copy-start.43 = (s32[2048]{0:T(1024)S(1)}, s32[2048]{0:T(1024)}, u32[]{:S(2)}) copy-start(s32[2048]{0:T(1024)} %param.11) | copy-start | bytes 24580
  78.3 24.8 %all-to-all-start.2 = ((bf16[2,1024,384]{1,2,0:T(8,128)(2,1)}), bf16[2,1024,384]{1,2,0:T(8,128)(2,1)}, u32[]{:S(2)}, u32[]{:S(2)}) async-start(bf16[2,1024,384]{1,2,0:T(8,128)(2,1)} %copy.199), calls=%async_computation.2 | async-start | bytes 3145728 | tf_op jit(solution)/shard_map/all_to_all | solution.py:299
  83.1 1.2 collective-permute-start.1
  119.3 110.7 %collective-permute-start.4 = (bf16[768,2112]{0,1:T(8,128)(2,1)}, bf16[768,2112]{0,1:T(8,128)(2,1)}, u32[]{:S(2)}, u32[]{:S(2)}) collective-permute-start(bf16[768,2112]{0,1:T(8,128)(2,1)} %copy.191), channel_id=1, source_target_pairs={{0,1},{1,0},{2,3},{3,2},{4,5},{5,4},{6,7},{7,6},{8,9},{9,8},{10,11... | collective-permute-start | bytes 9732104 | tf_op jit(solution)/shard_map/ppermute | solution.py:27
  225.2 17.3 %all-to-all-start = ((bf16[2,384,1024]{2,1,0:T(8,128)(2,1)}), bf16[2,384,1024]{2,1,0:T(8,128)(2,1)}, u32[]{:S(2)}, u32[]{:S(2)}) async-start(bf16[2,384,1024]{2,1,0:T(8,128)(2,1)} %bitcast.146), calls=%async_computation | async-start | bytes 3145728 | tf_op jit(solution)/shard_map/all_to_all | solution.py:299
  246.3 38.0 %copy-start.8 = (f32[1024,768]{0,1:T(8,128)}, f32[1024,768]{0,1:T(8,128)S(1)}, u32[]{:S(2)}) copy-start(f32[1024,768]{0,1:T(8,128)S(1)} %get-tuple-element.123) | copy-start | bytes 9437188
  271.5 6.5 copy-start.23
  297.3 16.9 %all-to-all-start.3 = ((bf16[2,384,1024]{2,1,0:T(8,128)(2,1)}), bf16[2,384,1024]{2,1,0:T(8,128)(2,1)}, u32[]{:S(2)}, u32[]{:S(2)}) async-start(bf16[2,384,1024]{2,1,0:T(8,128)(2,1)} %convolution_convert_fusion.1), calls=%async_computation.3 | async-start | bytes 3145728 | tf_op jit(solution)/shard_map/all_to_all | solution.py:299
  301.9 319.0 %reduce-scatter.7.cloned.1.call-start = ((), (), s32[]{:S(2)}) async-start(), calls=%async_computation.10 | async-start | bytes 2088960
  454.8 39.3 %collective-permute-start.5 = (bf16[6,64,2048]{2,1,0:T(8,128)(2,1)}, bf16[6,64,2048]{2,1,0:T(8,128)(2,1)}, u32[]{:S(2)}, u32[]{:S(2)}) collective-permute-start(bf16[6,64,2048]{2,1,0:T(8,128)(2,1)} %select_convert_fusion.1), channel_id=1, source_target_pairs={{0,2},{2,0},{4,6},{6,4},{8,10},{10,8},{12,14},{14,12},{16,18},{18,... | collective-permute-start | bytes 4718600 | tf_op jit(solution)/shard_map/ppermute | solution.py:27
  490.4 9.6 %collective-permute-start.6 = (bf16[6,64,2048]{2,1,0:T(8,128)(2,1)}, bf16[6,64,2048]{2,1,0:T(8,128)(2,1)}, u32[]{:S(2)}, u32[]{:S(2)}) collective-permute-start(bf16[6,64,2048]{2,1,0:T(8,128)(2,1)} %select_convert_fusion), channel_id=1, source_target_pairs={{0,2},{2,0},{4,6},{6,4},{8,10},{10,8},{12,14},{14,12},{16,18},{18,... | collective-permute-start | bytes 4718600 | tf_op jit(solution)/shard_map/ppermute | solution.py:27
  493.8 73.3 %collective-permute-start.8 = (bf16[768,2112]{0,1:T(8,128)(2,1)}, bf16[768,2112]{0,1:T(8,128)(2,1)}, u32[]{:S(2)}, u32[]{:S(2)}) collective-permute-start(bf16[768,2112]{0,1:T(8,128)(2,1)} %copy.217), channel_id=1, source_target_pairs={{0,1},{1,0},{2,3},{3,2},{4,5},{5,4},{6,7},{7,6},{8,9},{9,8},{10,11... | collective-permute-start | bytes 9732104 | tf_op jit(solution)/shard_map/ppermute | solution.py:27
  509.6 18.3 %copy-start.7 = (bf16[2048,768]{0,1:T(8,128)(2,1)}, bf16[2048,768]{0,1:T(8,128)(2,1)S(1)}, u32[]{:S(2)}) copy-start(bf16[2048,768]{0,1:T(8,128)(2,1)S(1)} %get-tuple-element.127) | copy-start | bytes 9437188
  527.9 133.4 %reduce-scatter.5.cloned.1.call-start = ((), (), s32[]{:S(2)}) async-start(), calls=%async_computation.9 | async-start | bytes 3551232 | tf_op jit(solution)/shard_map/reduce_scatter | solution.py:421
  529.2 71.7 %collective-permute-start.7 = (bf16[1024,768]{0,1:T(8,128)(2,1)}, bf16[1024,768]{0,1:T(8,128)(2,1)}, u32[]{:S(2)}, u32[]{:S(2)}) collective-permute-start(bf16[1024,768]{0,1:T(8,128)(2,1)} %broadcast_select_fusion.2), channel_id=1, source_target_pairs={{0,1},{1,0},{2,3},{3,2},{4,5},{5,4},{6,7},{7,6},{8,9},{9,8},{10,11... | collective-permute-start | bytes 4718600 | tf_op jit(solution)/shard_map/ppermute | solution.py:27
  584.1 33.1 %all-to-all-start.1 = ((bf16[2,1024,384]{1,2,0:T(8,128)(2,1)}), bf16[2,1024,384]{1,2,0:T(8,128)(2,1)S(1)}, u32[]{:S(2)}, u32[]{:S(2)}) async-start(bf16[2,1024,384]{1,2,0:T(8,128)(2,1)} %pad_maximum_fusion.17), calls=%async_computation.1 | async-start | bytes 3145728 | tf_op jit(solution)/shard_map/all_to_all | solution.py:299
  587.8 16.9 %copy-start.10 = (f32[1024,768]{0,1:T(8,128)S(1)}, f32[1024,768]{0,1:T(8,128)}, u32[]{:S(2)}) copy-start(f32[1024,768]{0,1:T(8,128)} %copy-done.9) | copy-start | bytes 9437188
  617.2 23.0 %all-to-all-start.4 = ((bf16[2,1024,384]{1,2,0:T(8,128)(2,1)}), bf16[2,1024,384]{1,2,0:T(8,128)(2,1)S(1)}, u32[]{:S(2)}, u32[]{:S(2)}) async-start(bf16[2,1024,384]{1,2,0:T(8,128)(2,1)} %pad_maximum_fusion.19), calls=%async_computation.4 | async-start | bytes 3145728 | tf_op jit(solution)/shard_map/all_to_all | solution.py:299
  623.0 19.8 %collective-permute-start.9 = (f32[2,48]{1,0:T(2,128)S(1)}, f32[2,48]{1,0:T(2,128)S(1)}, u32[]{:S(2)}, u32[]{:S(2)}) collective-permute-start(f32[2,48]{1,0:T(2,128)S(1)} %slice_bitcast_fusion.16), channel_id=1, source_target_pairs={{0,1},{1,0},{2,3},{3,2},{4,5},{5,4},{6,7},{7,6},{8,9},{9,8},{10,11... | collective-permute-start | bytes 1160 | tf_op jit(solution)/shard_map/ppermute | solution.py:27
  (34 other events, 116.1 us)
Sparse Core Ops, SparseCore 0:
  10.9 43.3 all-gather.2
  57.1 45.2 all-gather.4
  528.0 62.6 reduce-scatter.6
  594.4 66.8 reduce-scatter.4
